TPU v7x, 128 devices: a whole 4x4x4 slice. The times are simulated.
128 devices in a mesh: grp: 8 (over z_lo, y), blk: 16 (over x, z_hi, core).
Axes of the slice: x: 4, y: 4, z: 4 (z_hi: 2, z_lo: 2; z = z_hi * 2 + z_lo), core: 2. Of those that a mesh axis runs over, the one named last changes fastest.
Arguments:
- image_emb: bfloat16 [22528, 1152], P(('grp', 'blk')), may hold values from -16 to 16
- text_emb: bfloat16 [22528, 1152], P(('grp', 'blk')), may hold values from -16 to 16
- pair_ids: int32 [22528], P(('grp', 'blk')), may hold values from 0 to 703
- logit_scale: float32 [1], replicated, may hold values from 2.3 to 2.8
- bias: float32 [1], replicated, may hold values from -2.5 to -0.5
Outputs:
- image_grad: bfloat16 [22528, 1152], P(('grp', 'blk'))
- text_grad: bfloat16 [22528, 1152], P(('grp', 'blk'))
All inputs are finite; a program needn't handle non-finite values.
Results may differ from a plain program's by a relative error of at most 0.019.
Values may be sent and summed in bfloat16 or wider, within the bound.
A program may use at most 128 MiB of HBM per device.

v0:
```python
import functools
import math

import jax
import jax.numpy as jnp
from jax import lax
from jax.experimental import pallas as pl
from jax.experimental.pallas import tpu as pltpu
from jax.sharding import PartitionSpec as P

epsilon = 1e-06
MESH = pl.DeviceIdType.MESH
NT = (((1,), (1,)), ((), ()))
TN = (((0,), (0,)), ((), ()))
LOG2E = math.log2(math.e)


def places():
    g, b = lax.axis_index("grp"), lax.axis_index("blk")
    z_lo, y = g // 4, g % 4
    x, z_hi, core = b // 4, (b // 2) % 2, b % 2
    z = z_hi * 2 + z_lo

    def device(x, y, z, core):
        return ((z % 2) * 4 + y, x * 4 + (z // 2) * 2 + core)

    toward_a, toward_b = 3 - 2 * core, 1 + 2 * core
    text = dict(
        a=device((x + toward_a) % 4, y, z, core),
        b=device((x + toward_b) % 4, y, z, core),
        z=device(x, y, (z // 2) * 2 + 1 - z % 2, core),
    )
    image = dict(
        a=device(x, (y + toward_a) % 4, z, core),
        b=device(x, (y + toward_b) % 4, z, core),
        z=device(x, y, 3 - z, core),
    )
    return text, image, device(x, y, z, 1 - core), core


def unit_rows(embedding):
    values = embedding.astype(jnp.float32)
    inverse = lax.rsqrt(jnp.sum(values * values, axis=1, keepdims=True) + epsilon)
    return values * inverse, inverse


def kernel(rows, width, image_in, text_in, ids_in, scale_in, bias_in, image_out, text_out,
           texts, images, text_ids, image_ids, text_col, image_col, image_row, factors, text_acc, text_far, image_acc,
           sib_out, sib_in, text_send, text_recv, image_send, image_recv,
           gt_s, gt_r, gi_s, gi_r, gs_s, gs_r, ht_s, ht_r, hi_s, hi_r, hs_s, hs_r,
           rt_s, rt_r, ri_s, ri_r, rs_s, rs_r):
    pair = 2 * rows
    text_at, image_at, sibling, core = places()
    near_a, near_b, far_a, far_b = 3 - core, 2 + core, 6 - core, 5 + core

    barrier = pltpu.get_barrier_semaphore()
    partners = [*text_at.values(), *image_at.values(), sibling]
    for partner in partners:
        pl.semaphore_signal(barrier, inc=1, device_id=partner, device_id_type=MESH)

    scale = jnp.exp(scale_in[0])
    scale2, offset2 = scale * LOG2E, bias_in[0] * LOG2E

    def text_rows(k):
        return pl.ds(pl.multiple_of(k * pair, 16), rows)

    def sib_rows(k):
        return pl.ds(pl.multiple_of(k * pair + rows, 16), rows)

    def image_rows(k):
        return pl.ds(pl.multiple_of(k * rows, 16), rows)

    texts[text_rows(0), :] = unit_rows(text_in[...])[0].astype(jnp.bfloat16)
    images[image_rows(0), :] = unit_rows(image_in[...])[0].astype(jnp.bfloat16)
    for held in (text_ids, image_ids):
        held[0] = jnp.zeros((8, 256), jnp.int32)
        held[0, :, 0:rows] = jnp.broadcast_to(ids_in[...], (8, rows))
    pl.semaphore_wait(barrier, len(partners))

    sent = []

    def remote(src, dst, send, recv, to):
        return pltpu.make_async_remote_copy(
            src_ref=src, dst_ref=dst, send_sem=send, recv_sem=recv, device_id=to, device_id_type=MESH
        )

    def launch(copy):
        copy.start()
        sent.append(copy)

    def push_text(message, k, k_there, to, ids=True):
        launch(remote(texts.at[text_rows(k), :], texts.at[text_rows(k_there), :], gt_s.at[message], gt_r.at[message], to))
        if ids:
            launch(remote(text_ids.at[2 * k], text_ids.at[2 * k_there], ht_s.at[message], ht_r.at[message], to))

    def push_image(message, k, k_there, to, ids=True):
        launch(remote(images.at[image_rows(k), :], images.at[image_rows(k_there), :], gi_s.at[message], gi_r.at[message], to))
        if ids:
            launch(remote(image_ids.at[k], image_ids.at[k_there], hi_s.at[message], hi_r.at[message], to))

    def push_sibling(k):
        launch(remote(texts.at[text_rows(k), :], texts.at[sib_rows(k), :], gs_s.at[k], gs_r.at[k], sibling))
        launch(remote(text_ids.at[2 * k], text_ids.at[2 * k + 1], hs_s.at[k], hs_r.at[k], sibling))

    def took_text(message, k):
        place = texts.at[text_rows(k), :]
        remote(place, place, gt_s.at[message], gt_r.at[message], sibling).wait_recv()
        place = text_ids.at[2 * k]
        remote(place, place, ht_s.at[message], ht_r.at[message], sibling).wait_recv()

    def took_image(message, k):
        place = images.at[image_rows(k), :]
        remote(place, place, gi_s.at[message], gi_r.at[message], sibling).wait_recv()
        place = image_ids.at[k]
        remote(place, place, hi_s.at[message], hi_r.at[message], sibling).wait_recv()

    def took_sibling(k):
        place = texts.at[sib_rows(k), :]
        remote(place, place, gs_s.at[k], gs_r.at[k], sibling).wait_recv()
        place = text_ids.at[2 * k + 1]
        remote(place, place, hs_s.at[k], hs_r.at[k], sibling).wait_recv()

    def column(ids):
        return jnp.transpose(ids)[:rows, 0:1]

    def text_columns(blocks):
        for k in blocks:
            text_col[k * pair:k * pair + rows, :] = column(text_ids[2 * k])
            text_col[k * pair + rows:(k + 1) * pair, :] = column(text_ids[2 * k + 1])

    def image_columns(blocks):
        for k in blocks:
            image_col[k * rows:(k + 1) * rows, :] = column(image_ids[k])

    def image_window(first, last):
        for w in range(first, last, 128):
            image_row[:, w:w + 128] = jnp.transpose(jnp.broadcast_to(image_col[w:w + 128, :], (128, 128)))[0:8, :]

    def factor_strip(start, count, first, last):
        some = pl.ds(start, count)
        products = lax.dot_general(texts[some, :], images[first:last, :], NT, preferred_element_type=jnp.float32)
        e = jnp.exp2(products * scale2 + offset2)
        match = text_col[some, :] == image_row[0:1, first:last]
        factors[some, first:last] = (jnp.where(match, -1.0, e) * pltpu.reciprocal(1.0 + e, approx=True)).astype(jnp.bfloat16)

    def factor_block(start, blocks, first, last):
        def strip(n, carry):
            factor_strip(pl.multiple_of(start + n * pair, 16), pair, first, last)
            return carry

        lax.fori_loop(0, blocks, strip, 0)

    near_texts, near_images = 5 * pair, 768

    def text_pairs(k):
        return pl.ds(pl.multiple_of(k * pair, 16), pair)

    def to_sibling(k, part):
        sib_out[k] = part.astype(jnp.bfloat16)
        launch(remote(sib_out.at[k], sib_in.at[k], rs_s.at[k], rs_r.at[k], sibling))

    def early_text_gradients():
        def strip(k, carry):
            text_acc[text_pairs(k), :] = jnp.dot(
                factors[text_pairs(k), :near_images], images[:near_images, :], preferred_element_type=jnp.float32)
            return carry

        lax.fori_loop(0, 5, strip, 0)

    def text_gradient(k):
        part = jnp.dot(factors[text_pairs(k), near_images:], images[near_images:, :], preferred_element_type=jnp.float32)
        part = text_acc[text_pairs(k), :] + part
        text_acc[text_rows(k), :] = part[:rows]
        to_sibling(k, part[rows:])

    def far_text_gradient(k):
        part = jnp.dot(factors[text_pairs(k), :], images[...], preferred_element_type=jnp.float32)
        text_far[image_rows(k - 5), :] = part[:rows]
        to_sibling(k, part[rows:])

    def early_image_gradients(low, high):
        for first in range(low, high, 256):
            image_acc[first:first + 256, :] = lax.dot_general(
                factors[:near_texts, first:first + 256], texts[:near_texts, :], TN, preferred_element_type=jnp.float32)

    def image_gradient(first, last):
        image_acc[first:last, :] += lax.dot_general(
            factors[near_texts:, first:last], texts[near_texts:, :], TN, preferred_element_type=jnp.float32)

    def far_image_gradient(first, last):
        image_acc[first:last, :] = lax.dot_general(
            factors[:, first:last], texts[...], TN, preferred_element_type=jnp.float32)

    pieces = ((0, 96), (96, rows - 96))

    def piece_rows(start, p):
        return pl.ds(pl.multiple_of(start + pieces[p][0], 16), pieces[p][1])

    def wire(buffer, m, p):
        return buffer.at[m, pl.ds(*pieces[p]), :]

    def landed(buffer, sends, recvs, m, p):
        place = wire(buffer, m, p)
        remote(place, place, sends.at[p, m], recvs.at[p, m], sibling).wait_recv()
        return place[...].astype(jnp.float32)

    def text_sum(k, messages, p, far=False):
        if p == 0:
            remote(sib_in.at[k], sib_in.at[k], rs_s.at[k], rs_r.at[k], sibling).wait_recv()
        held = text_far[piece_rows((k - 5) * rows, p), :] if far else text_acc[piece_rows(k * pair, p), :]
        total = held + wire(sib_in, k, p)[...].astype(jnp.float32)
        for m in messages:
            total = total + landed(text_recv, rt_s, rt_r, m, p)
        return total

    def image_sum(k, messages, p):
        total = image_acc[piece_rows(k * rows, p), :]
        for m in messages:
            total = total + landed(image_recv, ri_s, ri_r, m, p)
        return total

    def text_hop(k, messages, m, to, far=False, some=(0, 1)):
        for p in some:
            wire(text_send, m, p)[...] = text_sum(k, messages, p, far).astype(jnp.bfloat16)
            launch(remote(wire(text_send, m, p), wire(text_recv, m, p), rt_s.at[p, m], rt_r.at[p, m], text_at[to]))

    def image_hop(k, messages, m, to, some=(0, 1)):
        for p in some:
            wire(image_send, m, p)[...] = image_sum(k, messages, p).astype(jnp.bfloat16)
            launch(remote(wire(image_send, m, p), wire(image_recv, m, p), ri_s.at[p, m], ri_r.at[p, m], image_at[to]))

    def finish(embedding, gradient):
        scaled, inverse = unit_rows(embedding)
        gradient = gradient * scale
        along = jnp.sum(scaled * gradient, axis=1, keepdims=True)
        return ((gradient - scaled * along) * inverse).astype(jnp.bfloat16)

    def text_done(p):
        some = pl.ds(*pieces[p])
        text_out[some, :] = finish(text_in[some, :], text_sum(0, (5, 6, 4), p))

    def image_done(p):
        some = pl.ds(*pieces[p])
        image_out[some, :] = finish(image_in[some, :], image_sum(0, (5, 6, 4), p))

    for m, k_there, to in ((1, near_a, "b"), (0, near_b, "a"), (2, 1, "z")):
        push_text(m, 0, k_there, text_at[to], False)
        push_image(m, 0, k_there, image_at[to], False)
    push_sibling(0)
    for m, k_there, to in ((1, near_a, "b"), (0, near_b, "a"), (2, 1, "z")):
        launch(remote(text_ids.at[0], text_ids.at[2 * k_there], ht_s.at[m], ht_r.at[m], text_at[to]))
        launch(remote(image_ids.at[0], image_ids.at[k_there], hi_s.at[m], hi_r.at[m], image_at[to]))

    took_text(1, near_a)
    push_text(3, near_a, 4, text_at["b"])
    took_image(1, near_a)
    push_image(3, near_a, 4, image_at["b"])
    took_text(2, 1)
    push_sibling(near_a)
    push_sibling(1)
    took_text(0, near_b)
    push_sibling(near_b)
    took_image(2, 1)
    took_image(0, near_b)
    image_columns([0, 1, 2, 3])
    image_window(0, 512)
    for k in (0, near_a, 1, near_b):
        took_sibling(k)
    text_columns([0, 1, 2, 3])
    factor_block(0, 4, 0, 512)

    took_text(3, 4)
    push_text(6, 4, 7, text_at["z"])
    push_text(4, 1, far_b, text_at["a"])
    push_text(5, 1, far_a, text_at["b"])
    took_image(3, 4)
    push_image(6, 4, 7, image_at["z"])
    push_image(4, 1, far_b, image_at["a"])
    push_image(5, 1, far_a, image_at["b"])
    push_sibling(4)
    image_columns([4])
    image_window(512, 768)
    took_sibling(4)
    text_columns([4])
    factor_block(0, 4, 512, 768)
    factor_block(4 * pair, 1, 0, 768)
    early_text_gradients()
    early_image_gradients(0, 512)

    took_text(4, far_b)
    push_sibling(far_b)
    took_text(5, far_a)
    push_sibling(far_a)
    took_text(6, 7)
    push_sibling(7)
    took_image(4, far_b)
    took_image(5, far_a)
    took_image(6, 7)
    early_image_gradients(512, 768)
    image_columns([5, 6, 7])
    image_window(768, 1408)
    for k in (far_b, far_a, 7):
        took_sibling(k)
    text_columns([5, 6, 7])

    factor_block(7 * pair, 1, 0, 1408)
    far_text_gradient(7)
    factor_block(5 * pair, 1, 0, 1408)
    text_hop(7, (), 0, "z", far=True)
    factor_block(6 * pair, 1, 0, 1408)
    image_gradient(256, 768)
    image_hop(near_b, (), 5, "b")
    far_text_gradient(5)
    far_text_gradient(6)
    factor_block(0, 2, 768, 1408)
    text_hop(far_a, (), 2, "a", far=True)
    text_hop(far_b, (), 3, "b", far=True)
    factor_block(2 * pair, 3, 768, 1408)
    far_image_gradient(1152, 1408)
    image_hop(7, (), 0, "z")
    far_image_gradient(768, 1152)
    image_hop(far_a, (), 2, "a")
    image_hop(far_b, (), 3, "b")
    text_gradient(4)
    text_gradient(2)
    text_hop(4, (0,), 1, "a")
    text_gradient(3)
    text_gradient(1)
    text_hop(near_b, (), 5, "b")
    image_gradient(0, 256)
    text_hop(1, (2, 3), 6, "z")
    image_hop(4, (0,), 1, "a", (0,))
    text_gradient(0)
    image_hop(4, (0,), 1, "a", (1,))
    image_hop(1, (2, 3), 6, "z", (0,))
    text_hop(near_a, (1,), 4, "a")
    image_hop(1, (2, 3), 6, "z", (1,))
    image_hop(near_a, (1,), 4, "a", (0,))
    image_hop(near_a, (1,), 4, "a", (1,))
    text_done(0)
    text_done(1)
    image_done(0)
    image_done(1)
    for copy in sent:
        copy.wait_send()


def local(image_emb, text_emb, pair_ids, logit_scale, bias):
    rows, width = image_emb.shape
    ids = pair_ids.reshape(1, rows)
    bf16, f32, i32 = jnp.bfloat16, jnp.float32, jnp.int32
    vmem, smem = pl.BlockSpec(memory_space=pltpu.VMEM), pl.BlockSpec(memory_space=pltpu.SMEM)
    dma = pltpu.SemaphoreType.DMA
    return pl.pallas_call(
        functools.partial(kernel, rows, width),
        out_shape=[jax.ShapeDtypeStruct((rows, width), bf16)] * 2,
        in_specs=[vmem, vmem, vmem, smem, smem],
        out_specs=[vmem, vmem],
        scratch_shapes=[
            pltpu.VMEM((16 * rows, width), bf16),
            pltpu.VMEM((8 * rows, width), bf16),
            pltpu.VMEM((16, 8, 256), i32),
            pltpu.VMEM((8, 8, 256), i32),
            pltpu.VMEM((16 * rows, 1), i32),
            pltpu.VMEM((8 * rows, 1), i32),
            pltpu.VMEM((8, 8 * rows), i32),
            pltpu.VMEM((16 * rows, 8 * rows), bf16),
            pltpu.VMEM((10 * rows, width), f32),
            pltpu.VMEM((3 * rows, width), f32),
            pltpu.VMEM((8 * rows, width), f32),
            pltpu.VMEM((8, rows, width), bf16),
            pltpu.VMEM((8, rows, width), bf16),
            pltpu.VMEM((7, rows, width), bf16),
            pltpu.VMEM((7, rows, width), bf16),
            pltpu.VMEM((7, rows, width), bf16),
            pltpu.VMEM((7, rows, width), bf16),
        ]
        + [dma((7,))] * 4 + [dma((8,))] * 2 + [dma((7,))] * 4 + [dma((8,))] * 2
        + [dma((2, 7))] * 4 + [dma((8,))] * 2,
        compiler_params=pltpu.CompilerParams(
            collective_id=0, has_side_effects=True, vmem_limit_bytes=63 << 20
        ),
    )(image_emb, text_emb, ids, logit_scale, bias)


def solution(mesh):
    placed = (P(("grp", "blk"), None), P(("grp", "blk"), None), P(("grp", "blk")), P(), P())
    return jax.shard_map(
        local,
        mesh=mesh,
        in_specs=placed,
        out_specs=(P(("grp", "blk"), None), P(("grp", "blk"), None)),
        check_vma=False,
    )
```

profile of v0, /device:TPU:1, one launch (start us, length us, event | category | flops | bytes accessed | tf_op | source)
XLA Modules:
  0.0 90.7 jit_solution(5032061341909177979)
XLA Ops:
  1.9 86.2 %shard_map.68 = (bf16[176,1152]{1,0:T(8,128)(2,1)}, bf16[176,1152]{1,0:T(8,128)(2,1)}) custom-call(bf16[176,1152]{1,0:T(8,128)(2,1)} %image_in.1, bf16[176,1152]{1,0:T(8,128)(2,1)} %text_in.1, s32[1,176]{1,0:T(1,128)} %bitcast.1, f32[1]{0:T(128)S(6)} %copy.9.scale_in, f32[1]{0:T(128)S(6)} %copy.10.bias_in), custom_call_target="tpu_custom_call" | custom-call | tf_op jit(solution)/shard_map/pallas_call | solution.py:354
  88.1 0.0 copy-start
  88.2 1.8 %copy.11 = bf16[176,1152]{1,0:T(8,128)(2,1)} copy(bf16[176,1152]{1,0:T(8,128)(2,1)} %get-tuple-element.4) | data formatting | bytes 811008
  90.0 0.0 copy-done
  90.0 0.8 copy.12
Async XLA Ops:
  88.1 1.8 %copy-start = (bf16[176,1152]{1,0:T(8,128)(2,1)S(1)}, bf16[176,1152]{1,0:T(8,128)(2,1)}, u32[]{:S(2)}) copy-start(bf16[176,1152]{1,0:T(8,128)(2,1)} %get-tuple-element.5) | copy-start | bytes 1216516
where the time goes:
time: 90.9 us; the launch traced here: 90.7 us
  Pallas kernels  86.2 us (95%)
  local copies, waits for them, and re-layouts  2.59 us (3%)
  between operations  1.94 us (2%)
    pallas_call x1, Pallas kernels, local(): pl.pallas_call(functools.partial(kernel, rows, width), out_shape=[jax.Sha...  86.2 us
    unnamed x4, local copies, waits for them, and re-layouts  2.59 us

commit v1 on v0

--- a/solution.py
+++ b/solution.py
@@ -88,37 +88,58 @@
         copy.start()
         sent.append(copy)
 
-    def push_text(message, k, k_there, to, ids=True):
-        launch(remote(texts.at[text_rows(k), :], texts.at[text_rows(k_there), :], gt_s.at[message], gt_r.at[message], to))
-        if ids:
-            launch(remote(text_ids.at[2 * k], text_ids.at[2 * k_there], ht_s.at[message], ht_r.at[message], to))
-
-    def push_image(message, k, k_there, to, ids=True):
-        launch(remote(images.at[image_rows(k), :], images.at[image_rows(k_there), :], gi_s.at[message], gi_r.at[message], to))
-        if ids:
-            launch(remote(image_ids.at[k], image_ids.at[k_there], hi_s.at[message], hi_r.at[message], to))
+    def push_text(m, k, k_there, to):
+        launch(remote(texts.at[text_rows(k), :], texts.at[text_rows(k_there), :], gt_s.at[m], gt_r.at[m], to))
+
+    def push_image(m, k, k_there, to):
+        launch(remote(images.at[image_rows(k), :], images.at[image_rows(k_there), :], gi_s.at[m], gi_r.at[m], to))
+
+    cuts = ((0, 96), (96, rows - 96))
+    second = {1: 7, 3: 8, 6: 9}
+
+    def text_cut(k, p):
+        return pl.ds(pl.multiple_of(k * pair + cuts[p][0], 16), cuts[p][1])
+
+    def image_cut(k, p):
+        return pl.ds(pl.multiple_of(k * rows + cuts[p][0], 16), cuts[p][1])
+
+    def push_cuts(m, k, k_there, to, some=(0, 1)):
+        for p in some:
+            i = m if p == 0 else second[m]
+            launch(remote(texts.at[text_cut(k, p), :], texts.at[text_cut(k_there, p), :], gt_s.at[i], gt_r.at[i], text_at[to]))
+            launch(remote(images.at[image_cut(k, p), :], images.at[image_cut(k_there, p), :], gi_s.at[i], gi_r.at[i], image_at[to]))
+
+    def took_cut(m, k, p):
+        i = m if p == 0 else second[m]
+        took(texts.at[text_cut(k, p), :], gt_s.at[i], gt_r.at[i])
+        took(images.at[image_cut(k, p), :], gi_s.at[i], gi_r.at[i])
 
     def push_sibling(k):
         launch(remote(texts.at[text_rows(k), :], texts.at[sib_rows(k), :], gs_s.at[k], gs_r.at[k], sibling))
+
+    def took(place, send, recv):
+        remote(place, place, send, recv, sibling).wait_recv()
+
+    def took_text(m, k):
+        took(texts.at[text_rows(k), :], gt_s.at[m], gt_r.at[m])
+
+    def took_image(m, k):
+        took(images.at[image_rows(k), :], gi_s.at[m], gi_r.at[m])
+
+    def took_sibling(k):
+        took(texts.at[sib_rows(k), :], gs_s.at[k], gs_r.at[k])
+
+    def push_ids(m, k, k_there, to):
+        launch(remote(text_ids.at[2 * k], text_ids.at[2 * k_there], ht_s.at[m], ht_r.at[m], text_at[to]))
+        launch(remote(image_ids.at[k], image_ids.at[k_there], hi_s.at[m], hi_r.at[m], image_at[to]))
+
+    def push_sibling_ids(k):
         launch(remote(text_ids.at[2 * k], text_ids.at[2 * k + 1], hs_s.at[k], hs_r.at[k], sibling))
 
-    def took_text(message, k):
-        place = texts.at[text_rows(k), :]
-        remote(place, place, gt_s.at[message], gt_r.at[message], sibling).wait_recv()
-        place = text_ids.at[2 * k]
-        remote(place, place, ht_s.at[message], ht_r.at[message], sibling).wait_recv()
-
-    def took_image(message, k):
-        place = images.at[image_rows(k), :]
-        remote(place, place, gi_s.at[message], gi_r.at[message], sibling).wait_recv()
-        place = image_ids.at[k]
-        remote(place, place, hi_s.at[message], hi_r.at[message], sibling).wait_recv()
-
-    def took_sibling(k):
-        place = texts.at[sib_rows(k), :]
-        remote(place, place, gs_s.at[k], gs_r.at[k], sibling).wait_recv()
-        place = text_ids.at[2 * k + 1]
-        remote(place, place, hs_s.at[k], hs_r.at[k], sibling).wait_recv()
+    def took_ids(m, k):
+        took(text_ids.at[2 * k], ht_s.at[m], ht_r.at[m])
+        took(image_ids.at[k], hi_s.at[m], hi_r.at[m])
+        push_sibling_ids(k)
 
     def column(ids):
         return jnp.transpose(ids)[:rows, 0:1]
@@ -159,17 +180,8 @@
         sib_out[k] = part.astype(jnp.bfloat16)
         launch(remote(sib_out.at[k], sib_in.at[k], rs_s.at[k], rs_r.at[k], sibling))
 
-    def early_text_gradients():
-        def strip(k, carry):
-            text_acc[text_pairs(k), :] = jnp.dot(
-                factors[text_pairs(k), :near_images], images[:near_images, :], preferred_element_type=jnp.float32)
-            return carry
-
-        lax.fori_loop(0, 5, strip, 0)
-
     def text_gradient(k):
-        part = jnp.dot(factors[text_pairs(k), near_images:], images[near_images:, :], preferred_element_type=jnp.float32)
-        part = text_acc[text_pairs(k), :] + part
+        part = jnp.dot(factors[text_pairs(k), :], images[...], preferred_element_type=jnp.float32)
         text_acc[text_rows(k), :] = part[:rows]
         to_sibling(k, part[rows:])
 
@@ -243,65 +255,78 @@
         some = pl.ds(*pieces[p])
         image_out[some, :] = finish(image_in[some, :], image_sum(0, (5, 6, 4), p))
 
-    for m, k_there, to in ((1, near_a, "b"), (0, near_b, "a"), (2, 1, "z")):
-        push_text(m, 0, k_there, text_at[to], False)
-        push_image(m, 0, k_there, image_at[to], False)
+    own_to = ((1, near_a, "b"), (0, near_b, "a"), (2, 1, "z"))
+    for m, k_there, to in own_to:
+        push_ids(m, 0, k_there, to)
+    push_sibling_ids(0)
+    push_cuts(1, 0, near_a, "b")
+    for m, k_there, to in own_to[1:]:
+        push_text(m, 0, k_there, text_at[to])
+        push_image(m, 0, k_there, image_at[to])
     push_sibling(0)
-    for m, k_there, to in ((1, near_a, "b"), (0, near_b, "a"), (2, 1, "z")):
-        launch(remote(text_ids.at[0], text_ids.at[2 * k_there], ht_s.at[m], ht_r.at[m], text_at[to]))
-        launch(remote(image_ids.at[0], image_ids.at[k_there], hi_s.at[m], hi_r.at[m], image_at[to]))
-
-    took_text(1, near_a)
-    push_text(3, near_a, 4, text_at["b"])
-    took_image(1, near_a)
-    push_image(3, near_a, 4, image_at["b"])
+    took_ids(1, near_a)
+    push_ids(3, near_a, 4, "b")
+    took_ids(2, 1)
+    push_ids(4, 1, far_b, "a")
+    push_ids(5, 1, far_a, "b")
+    took_ids(0, near_b)
+    for k in (0, near_a, 1, near_b):
+        took(text_ids.at[2 * k + 1], hs_s.at[k], hs_r.at[k])
+    text_columns([0, 1, 2, 3])
+    image_columns([0, 1, 2, 3])
+    image_window(0, 512)
+
+    took_cut(1, near_a, 0)
+    push_cuts(3, near_a, 4, "b", (0,))
+    took_cut(1, near_a, 1)
+    push_cuts(3, near_a, 4, "b", (1,))
     took_text(2, 1)
+    push_text(4, 1, far_b, text_at["a"])
+    push_text(5, 1, far_a, text_at["b"])
+    took_image(2, 1)
+    push_image(4, 1, far_b, image_at["a"])
+    push_image(5, 1, far_a, image_at["b"])
     push_sibling(near_a)
     push_sibling(1)
     took_text(0, near_b)
     push_sibling(near_b)
-    took_image(2, 1)
     took_image(0, near_b)
-    image_columns([0, 1, 2, 3])
-    image_window(0, 512)
+    took_ids(3, 4)
+    push_ids(6, 4, 7, "z")
+    took_cut(3, 4, 0)
+    push_cuts(6, 4, 7, "z", (0,))
     for k in (0, near_a, 1, near_b):
         took_sibling(k)
-    text_columns([0, 1, 2, 3])
     factor_block(0, 4, 0, 512)
 
-    took_text(3, 4)
-    push_text(6, 4, 7, text_at["z"])
-    push_text(4, 1, far_b, text_at["a"])
-    push_text(5, 1, far_a, text_at["b"])
-    took_image(3, 4)
-    push_image(6, 4, 7, image_at["z"])
-    push_image(4, 1, far_b, image_at["a"])
-    push_image(5, 1, far_a, image_at["b"])
+    took_cut(3, 4, 1)
+    push_cuts(6, 4, 7, "z", (1,))
     push_sibling(4)
-    image_columns([4])
-    image_window(512, 768)
+    took_ids(4, far_b)
+    took_ids(5, far_a)
+    took_ids(6, 7)
+    for k in (4, far_b, far_a, 7):
+        took(text_ids.at[2 * k + 1], hs_s.at[k], hs_r.at[k])
+    text_columns([4, 5, 6, 7])
+    image_columns([4, 5, 6, 7])
+    image_window(512, 1408)
     took_sibling(4)
-    text_columns([4])
     factor_block(0, 4, 512, 768)
     factor_block(4 * pair, 1, 0, 768)
-    early_text_gradients()
     early_image_gradients(0, 512)
 
     took_text(4, far_b)
     push_sibling(far_b)
     took_text(5, far_a)
     push_sibling(far_a)
-    took_text(6, 7)
+    took_cut(6, 7, 0)
+    took_cut(6, 7, 1)
     push_sibling(7)
     took_image(4, far_b)
     took_image(5, far_a)
-    took_image(6, 7)
     early_image_gradients(512, 768)
-    image_columns([5, 6, 7])
-    image_window(768, 1408)
     for k in (far_b, far_a, 7):
         took_sibling(k)
-    text_columns([5, 6, 7])
 
     factor_block(7 * pair, 1, 0, 1408)
     far_text_gradient(7)
@@ -325,17 +350,17 @@
     text_gradient(2)
     text_hop(4, (0,), 1, "a")
     text_gradient(3)
+    text_hop(near_b, (), 5, "b")
+    image_hop(4, (0,), 1, "a", (0,))
     text_gradient(1)
-    text_hop(near_b, (), 5, "b")
+    image_hop(4, (0,), 1, "a", (1,))
     image_gradient(0, 256)
     text_hop(1, (2, 3), 6, "z")
-    image_hop(4, (0,), 1, "a", (0,))
+    image_hop(1, (2, 3), 6, "z", (0,))
     text_gradient(0)
-    image_hop(4, (0,), 1, "a", (1,))
-    image_hop(1, (2, 3), 6, "z", (0,))
-    text_hop(near_a, (1,), 4, "a")
     image_hop(1, (2, 3), 6, "z", (1,))
     image_hop(near_a, (1,), 4, "a", (0,))
+    text_hop(near_a, (1,), 4, "a")
     image_hop(near_a, (1,), 4, "a", (1,))
     text_done(0)
     text_done(1)
@@ -375,7 +400,7 @@
             pltpu.VMEM((7, rows, width), bf16),
             pltpu.VMEM((7, rows, width), bf16),
         ]
-        + [dma((7,))] * 4 + [dma((8,))] * 2 + [dma((7,))] * 4 + [dma((8,))] * 2
+        + [dma((10,))] * 4 + [dma((8,))] * 2 + [dma((7,))] * 4 + [dma((8,))] * 2
         + [dma((2, 7))] * 4 + [dma((8,))] * 2,
         compiler_params=pltpu.CompilerParams(
             collective_id=0, has_side_effects=True, vmem_limit_bytes=63 << 20

time: 90.9 us -> 90.7 us (level)
  no operation moved by 1% of the time
where the time goes in v1:
time: 90.7 us; the launch traced here: 90.6 us
  Pallas kernels  86 us (95%)
  local copies, waits for them, and re-layouts  2.59 us (3%)
  between operations  1.94 us (2%)
    pallas_call x1, Pallas kernels, local(): pl.pallas_call(functools.partial(kernel, rows, width), out_shape=[jax.Sha...  86 us
    unnamed x4, local copies, waits for them, and re-layouts  2.59 us

profile of v1, /device:TPU:1, one launch (start us, length us, event | category | flops | bytes accessed | tf_op | source)
XLA Modules:
  0.0 90.6 jit_solution(3573235121184629946)
XLA Ops:
  1.9 86.0 %shard_map.68 = (bf16[176,1152]{1,0:T(8,128)(2,1)}, bf16[176,1152]{1,0:T(8,128)(2,1)}) custom-call(bf16[176,1152]{1,0:T(8,128)(2,1)} %image_in.1, bf16[176,1152]{1,0:T(8,128)(2,1)} %text_in.1, s32[1,176]{1,0:T(1,128)} %bitcast.1, f32[1]{0:T(128)S(6)} %copy.9.scale_in, f32[1]{0:T(128)S(6)} %copy.10.bias_in), custom_call_target="tpu_custom_call" | custom-call | tf_op jit(solution)/shard_map/pallas_call | solution.py:379
  88.0 0.0 copy-start
  88.0 1.8 %copy.11 = bf16[176,1152]{1,0:T(8,128)(2,1)} copy(bf16[176,1152]{1,0:T(8,128)(2,1)} %get-tuple-element.4) | data formatting | bytes 811008
  89.8 0.0 copy-done
  89.8 0.8 copy.12
Async XLA Ops:
  88.0 1.8 %copy-start = (bf16[176,1152]{1,0:T(8,128)(2,1)S(1)}, bf16[176,1152]{1,0:T(8,128)(2,1)}, u32[]{:S(2)}) copy-start(bf16[176,1152]{1,0:T(8,128)(2,1)} %get-tuple-element.5) | copy-start | bytes 1216516
